TPU v7x, 32 devices: a whole 2x2x4 slice. The times are simulated.
32 devices in a mesh: expert: 8 (over z, x), tensor: 4 (over y, core).
Axes of the slice: x: 2, y: 2, z: 4, core: 2. Of those that a mesh axis runs over, the one named last changes fastest.
Arguments:
- query_latent: bfloat16 [256, 64, 576], P(('expert', 'tensor')), may hold values from -9 to 9
- kv_cache: bfloat16 [256, 768, 576], P(('expert', 'tensor')), may hold values from -4 to 4
- cache_len: int32 [256], P(('expert', 'tensor')), may hold values from 192 to 768, as said below
- value_up: bfloat16 [64, 512, 128], P('tensor'), may hold values from -0.25 to 0.25
- hidden_in: bfloat16 [256, 7168], P('expert', 'tensor'), may hold values from -6 to 6
- norm_gain: bfloat16 [7168], P('tensor'), may hold values from 0.099609375 to 1.8984375
- expert_ids: int32 [256, 8], P('expert'), may hold values from 0 to 7, all different within a row; in each aligned block of 32 rows (0 to 31, 32 to 63, ...) at most 32 rows name the same one
- route_weight: int32 [256, 8], P('expert'), may hold values from 1 to 4095
- placement_plan: int32 [8], replicated, may hold values from 0 to 7, as said below
- updated_list: int32 [8], replicated, may hold values from 0 to 7, each once
- learner_gate: bfloat16 [8, 7168, 1024], P(None, 'expert', 'tensor'), may hold values from -0.0625 to 0.0625
- learner_up: bfloat16 [8, 7168, 1024], P(None, 'expert', 'tensor'), may hold values from -0.0625 to 0.0625
- learner_down: bfloat16 [8, 7168, 1024], P(None, 'expert', 'tensor'), may hold values from -0.1875 to 0.1875
Outputs:
- attn_values: bfloat16 [256, 8192], P('expert', 'tensor')
- moe_out: bfloat16 [256, 7168], P('expert', 'tensor')
- slot_gate: bfloat16 [8, 7168, 1024], P('expert', None, 'tensor')
Inputs may be any that keep to these rules, and one draw needn't show every extreme that they name: `cache_len`: some row has all 768 positions valid. `placement_plan`: every expert is held by one or two slots; 0 experts by two. `expert_ids`: each row names 8 different experts; among the 32 rows of one device no expert is named more than 32 times. `updated_list`: each expert once.
All inputs are finite; a program needn't handle non-finite values.
Results may differ from a plain program's by a relative error of at most 0.015.
Values may be sent and summed in bfloat16 or wider, within the bound.
A program may use at most 128 MiB of HBM per device.

v0:
```python
import jax
import jax.numpy as jnp
from jax import lax
from jax.sharding import PartitionSpec as P

KVL = 512


SCORE_SCALE = 192.0 ** (-0.5)
ROUTE_SCALE = 2.5
NORM_EPSILON = 1e-06


def attend(query_latent, kv_cache, cache_len):
    scores = (
        jnp.einsum("rhc,rpc->rhp", query_latent, kv_cache, preferred_element_type=jnp.float32)
        * SCORE_SCALE
    )
    allowed = (jnp.arange(kv_cache.shape[1], dtype=jnp.int32)[None, :] < cache_len[:, None])[
        :, None, :
    ]
    scores = jnp.where(allowed, scores, -1e30)
    highest = jnp.max(scores, axis=2, keepdims=True)
    lifted = jnp.where(allowed, jnp.exp(scores - highest), 0.0)
    totals = jnp.sum(lifted, axis=2, keepdims=True)
    mixed = jnp.einsum(
        "rhp,rpc->rhc",
        lifted.astype(jnp.bfloat16),
        kv_cache[:, :, :KVL],
        preferred_element_type=jnp.float32,
    )
    return (mixed / totals).astype(jnp.bfloat16)


def route_targets(expert_ids, placement_plan, expert_total, capacity):
    row_count, choose_count = expert_ids.shape
    entries = row_count * choose_count
    slot_total = placement_plan.shape[0]
    flat_ids = expert_ids.reshape(entries)
    expert_range = jnp.arange(expert_total, dtype=jnp.int32)
    holders = (placement_plan[None, :] == expert_range[:, None]).astype(jnp.int32)
    holder_rank = jnp.cumsum(holders, axis=1) - 1
    picked = (flat_ids[:, None] == expert_range[None, :]).astype(jnp.int32)
    entry_hold = jnp.dot(picked, holders)
    entry_rank = jnp.dot(picked, holder_rank)
    matched = entry_hold * (entry_rank == 0).astype(jnp.int32)
    slot_index = jnp.sum(matched * jnp.arange(slot_total, dtype=jnp.int32)[None, :], axis=1)
    position = jnp.sum(matched * (jnp.cumsum(matched, axis=0) - 1), axis=1)
    return slot_index * capacity + position


def per_device(
    query_latent,
    kv_cache,
    cache_len,
    value_up,
    hidden_in,
    norm_gain,
    expert_ids,
    route_weight,
    placement_plan,
    updated_list,
    learner_gate,
    learner_up,
    learner_down,
):
    expert_total = updated_list.shape[0]
    entry_range = jnp.arange(expert_total, dtype=jnp.int32)
    learner_entry = jnp.sum(
        entry_range[None, :] * (updated_list[None, :] == placement_plan[:, None]).astype(jnp.int32),
        axis=1,
    )
    held_gate, held_up = (
        lax.all_to_all(
            jnp.take(learner_gate, learner_entry, axis=0),
            "expert",
            split_axis=0,
            concat_axis=1,
            tiled=True,
        ),
        lax.all_to_all(
            jnp.take(learner_up, learner_entry, axis=0),
            "expert",
            split_axis=0,
            concat_axis=1,
            tiled=True,
        ),
    )
    chosen_down = jnp.take(learner_down, learner_entry, axis=0)
    held_down = lax.all_to_all(chosen_down, "expert", split_axis=0, concat_axis=1, tiled=True)
    latent = attend(query_latent, kv_cache, cache_len)
    head_rows = lax.all_to_all(latent, "tensor", split_axis=1, concat_axis=0, tiled=True)
    projected = jnp.einsum("rhc,hcv->rhv", head_rows, value_up, preferred_element_type=jnp.float32)
    attn_values = projected.astype(jnp.bfloat16).reshape(
        head_rows.shape[0], projected.shape[1] * projected.shape[2]
    )
    row_count, choose_count = expert_ids.shape
    slot_total = placement_plan.shape[0]
    capacity = min(row_count, 2 * ((row_count * choose_count + expert_total - 1) // expert_total))
    targets = route_targets(expert_ids, placement_plan, expert_total, capacity)
    entry_row = jnp.arange(row_count * choose_count, dtype=jnp.int32) // choose_count
    whole_rows, whole_gain = (
        lax.all_gather(hidden_in, "tensor", axis=1, tiled=True),
        lax.all_gather(norm_gain.reshape(1, norm_gain.shape[0]), "tensor", axis=1, tiled=True),
    )
    widened = whole_rows.astype(jnp.float32)
    normed = (
        widened
        * lax.rsqrt(jnp.mean(widened * widened, axis=1, keepdims=True) + NORM_EPSILON)
        * whole_gain.astype(jnp.float32)
    ).astype(jnp.bfloat16)
    outbound = (
        jnp.zeros((slot_total * capacity, normed.shape[1]), jnp.bfloat16)
        .at[targets]
        .set(normed[entry_row])
    )
    arrived = lax.all_to_all(outbound, "expert", split_axis=0, concat_axis=0, tiled=True)
    gate_proj = jnp.dot(arrived, held_gate[0], preferred_element_type=jnp.float32)
    up_proj = jnp.dot(arrived, held_up[0], preferred_element_type=jnp.float32)
    activated = (jax.nn.silu(gate_proj) * up_proj).astype(jnp.bfloat16)
    partial_out = lax.dot_general(
        activated, held_down[0], (((1,), (1,)), ((), ())), preferred_element_type=jnp.float32
    )
    shared = lax.psum_scatter(
        partial_out.astype(jnp.bfloat16), "tensor", scatter_dimension=1, tiled=True
    )
    returned = lax.all_to_all(shared, "expert", split_axis=0, concat_axis=0, tiled=True)
    entry_out = (
        returned[targets].astype(jnp.float32).reshape(row_count, choose_count, returned.shape[1])
    )
    weights_float = route_weight.astype(jnp.float32)
    gates = ROUTE_SCALE * weights_float / jnp.sum(weights_float, axis=1, keepdims=True)
    moe_out = jnp.sum(gates[:, :, None] * entry_out, axis=1).astype(jnp.bfloat16)
    return (attn_values, moe_out, held_gate)


def solution(mesh):
    in_specs = (
        P(("expert", "tensor"), None, None),
        P(("expert", "tensor"), None, None),
        P(("expert", "tensor")),
        P("tensor", None, None),
        P("expert", "tensor"),
        P("tensor"),
        P("expert", None),
        P("expert", None),
        P(),
        P(),
        P(None, "expert", "tensor"),
        P(None, "expert", "tensor"),
        P(None, "expert", "tensor"),
    )
    out_specs = (P("expert", "tensor"), P("expert", "tensor"), P("expert", None, "tensor"))
    return jax.shard_map(
        per_device, mesh=mesh, in_specs=in_specs, out_specs=out_specs, check_vma=False
    )
```

profile of v0, /device:TPU:27, one launch (start us, length us, event | category | flops | bytes accessed | tf_op | source)
XLA Modules:
  0.0 483.3 jit_solution(1467791165964958019)
XLA Ops:
  11.1 7.6 %all_gather.6 = bf16[32,7168]{1,0:T(8,128)(2,1)S(1)} all-gather(bf16[32,1792]{1,0:T(8,128)(2,1)} %param.19), channel_id=1, replica_groups=mesh['expert'=8,'tensor'=4] {'tensor'}, dimensions={1}, use_global_device_ids=true | all-gather | bytes 573440 | tf_op jit(solution)/shard_map/all_gather | solution.py:103
  19.6 5.2 %all-gather.1 = bf16[4,1,1792]{2,1,0:T(2,128)(2,1)S(1)} all-gather(bf16[1,1,1792]{2,1,0:T(2,128)(2,1)S(1)} %reshape.212), channel_id=2, replica_groups=mesh['expert'=8,'tensor'=4] {'tensor'}, dimensions={0}, use_global_device_ids=true | all-gather | bytes 17920 | tf_op jit(solution)/shard_map/all_gather | solution.py:104
  25.0 18.3 %scatter_custom_fusion = bf16[256,7168]{1,0:T(8,128)(2,1)} fusion(s32[256]{0:T(256)S(1)} %bitcast.55, bf16[32,7168]{1,0:T(8,128)(2,1)S(1)} %fusion.14, s32[1024]{0:T(1024)S(1)} %pad_clamp_fusion.2, bf16[]{:T(256)} %constant.56.clone.1), kind=kCustom, calls=%fused_computation.10 | custom fusion | bytes 3670018 | tf_op jit(solution)/shard_map/scatter | solution.py:115
  43.3 5.6 %all-to-all-start.1 = ((bf16[8,32,7168]{2,1,0:T(8,128)(2,1)}), bf16[8,32,7168]{2,1,0:T(8,128)(2,1)}, u32[]{:S(2)}, u32[]{:S(2)}) async-start(bf16[8,32,7168]{2,1,0:T(8,128)(2,1)} %bitcast.49), calls=%async_computation.1 | async-start | bytes 7340032 | tf_op jit(solution)/shard_map/all_to_all | solution.py:117
  49.1 4.7 gather_fusion.1
  53.7 4.7 gather_fusion.2
  58.5 4.6 gather_fusion.3
  63.1 7.8 %broadcast_select_fusion.2 = (bf16[8,896,256]{2,1,0:T(8,128)(2,1)}, bf16[8,896,256]{2,1,0:T(8,128)(2,1)}, bf16[8,896,256]{2,1,0:T(8,128)(2,1)}) fusion(bf16[8,896,256]{2,1,0:T(8,128)(2,1)} %gather_fusion.1, pred[8]{0:T(512)(128)(4,1)S(1)} %compare_and_fusion, bf16[8,896,256]{2,1,0:T(8,128)(2,1)} %gather_fusion.2, bf16[8,896,256]{2,1,0:T(8,128)(2,1)} %gather_fusion.3), kind=kLoop, calls=%fused_computation.14 | loop fusion | flops 5505024 | bytes 22020104 | tf_op jit(solution)/shard_map/jit(_take)/select_n | solution.py:75
  70.8 58.5 %all-to-all-done.1 = bf16[8,32,7168]{2,1,0:T(8,128)(2,1)} async-done(((bf16[8,32,7168]{2,1,0:T(8,128)(2,1)}), bf16[8,32,7168]{2,1,0:T(8,128)(2,1)}, u32[]{:S(2)}, u32[]{:S(2)}) %all-to-all-start.1) | async-done | bytes 3670048 | tf_op jit(solution)/shard_map/all_to_all | solution.py:117
  129.3 85.6 %all_to_all.72 = bf16[8,896,256]{2,1,0:T(8,128)(2,1)} all-to-all(bf16[8,896,256]{2,1,0:T(8,128)(2,1)} %get-tuple-element.6), channel_id=1, replica_groups=mesh['expert'=8,'tensor'=4] {'expert'}, dimensions={0} | all-to-all | bytes 7340032 | tf_op jit(solution)/shard_map/all_to_all | solution.py:74
  214.9 84.9 %all_to_all.73 = bf16[8,896,256]{2,1,0:T(8,128)(2,1)} all-to-all(bf16[8,896,256]{2,1,0:T(8,128)(2,1)S(1)} %copy-done.1), channel_id=1, replica_groups=mesh['expert'=8,'tensor'=4] {'expert'}, dimensions={0} | all-to-all | bytes 7340032 | tf_op jit(solution)/shard_map/all_to_all | solution.py:81
  299.8 5.9 %all-to-all-start.4 = ((bf16[8,896,256]{2,1,0:T(8,128)(2,1)}), bf16[8,896,256]{2,1,0:T(8,128)(2,1)}, u32[]{:S(2)}, u32[]{:S(2)}) async-start(bf16[8,896,256]{2,1,0:T(8,128)(2,1)} %get-tuple-element.8), calls=%async_computation.4 | async-start | bytes 7340032 | tf_op jit(solution)/shard_map/all_to_all | solution.py:90
  305.7 4.3 fusion.34
  310.0 76.1 %all-to-all-done.4 = bf16[8,896,256]{2,1,0:T(8,128)(2,1)} async-done(((bf16[8,896,256]{2,1,0:T(8,128)(2,1)}), bf16[8,896,256]{2,1,0:T(8,128)(2,1)}, u32[]{:S(2)}, u32[]{:S(2)}) %all-to-all-start.4) | async-done | bytes 3670048 | tf_op jit(solution)/shard_map/all_to_all | solution.py:90
  386.1 10.0 %convolution_convert_fusion = bf16[256,7168]{1,0:T(8,128)(2,1)} fusion(bf16[7168,256]{1,0:T(8,128)(2,1)} %bitcast.16, bf16[256,7168]{1,0:T(8,128)(2,1)} %bitcast.13, bf16[7168,256]{1,0:T(8,128)(2,1)} %bitcast.46, f32[256,256]{1,0:T(8,128)S(1)} %fusion.34), kind=kOutput, calls=%fused_computation.7 | convolution fusion | flops 1881276416 | bytes 14942208 | tf_op jit(solution)/shard_map/dot_general | solution.py:121
  397.2 4.7 fusion.33
  402.0 5.4 %divide_convert_fusion = bf16[8,64,512]{2,1,0:T(8,128)(2,1)S(1)} fusion(bf16[8,768,576]{1,2,0:T(8,128)(2,1)} %param.16, bf16[8,64,768]{2,1,0:T(8,128)(2,1)S(1)} %get-tuple-element.10, f32[8,64]{1,0:T(8,128)S(1)} %get-tuple-element.9), kind=kOutput, calls=%fused_computation.29 | convolution fusion | flops 403177472 | bytes 7604224 | tf_op jit(solution)/shard_map/rhp,rpc->rhc/dot_general | solution.py:26
  407.7 12.5 %all_to_all.74 = bf16[8,64,512]{2,0,1:T(8,128)(2,1)S(1)} all-to-all(bf16[8,64,512]{2,0,1:T(8,128)(2,1)S(1)} %copy.31), channel_id=1, replica_groups=mesh['expert'=8,'tensor'=4] {'tensor'}, dimensions={1} | all-to-all | bytes 1048576 | tf_op jit(solution)/shard_map/all_to_all | solution.py:92
  420.1 19.8 %reduce-scatter.2.cloned.1.call-done = bf16[256,1792]{1,0:T(8,128)(2,1)} async-done(((bf16[256,7168]{1,0:T(8,128)(2,1)}), bf16[256,1792]{1,0:T(8,128)(2,1)}) %reduce-scatter.2.cloned.1.call-update) | async-done | bytes 917520 | tf_op jit(solution)/shard_map/reduce_scatter | solution.py:124
  439.9 6.0 %all-to-all-start.5 = ((bf16[8,32,1792]{2,1,0:T(8,128)(2,1)}), bf16[8,32,1792]{2,1,0:T(8,128)(2,1)S(1)}, u32[]{:S(2)}, u32[]{:S(2)}) async-start(bf16[8,32,1792]{2,1,0:T(8,128)(2,1)} %bitcast.51), calls=%async_computation.6 | async-start | bytes 1835008 | tf_op jit(solution)/shard_map/all_to_all | solution.py:127
  449.7 17.5 %all-to-all-done.5 = bf16[8,32,1792]{2,1,0:T(8,128)(2,1)S(1)} async-done(((bf16[8,32,1792]{2,1,0:T(8,128)(2,1)}), bf16[8,32,1792]{2,1,0:T(8,128)(2,1)S(1)}, u32[]{:S(2)}, u32[]{:S(2)}) %all-to-all-start.5) | async-done | bytes 917536 | tf_op jit(solution)/shard_map/all_to_all | solution.py:127
  467.2 2.4 gather_fusion
  469.6 2.7 fusion.5
  472.4 4.1 copy.45
  (50 shorter events, 10.4 us)
Async XLA Ops:
  7.2 441.4 %copy-start = (bf16[16,512,128]{2,1,0:T(8,128)(2,1)S(1)}, bf16[16,512,128]{2,1,0:T(8,128)(2,1)}, u32[]{:S(2)}) copy-start(bf16[16,512,128]{2,1,0:T(8,128)(2,1)} %param.18) | copy-start | bytes 6291460
  11.1 32.2 %copy-start.3 = (s32[256,1]{0,1:T(1,128)}, s32[256,1]{0,1:T(1,128)S(1)}, u32[]{:S(2)}) copy-start(s32[256,1]{0,1:T(1,128)S(1)} %compare_select_fusion.1) | copy-start | bytes 3076
  43.3 5.6 %copy-start.4 = (s32[8]{0:T(128)S(1)}, s32[8]{0:T(128)}, u32[]{:S(2)}) copy-start(s32[8]{0:T(128)} %param.23) | copy-start | bytes 100
  43.3 5.6 %copy-start.7 = (s32[8]{0:T(128)S(1)}, s32[8]{0:T(128)}, u32[]{:S(2)}) copy-start(s32[8]{0:T(128)} %param.24) | copy-start | bytes 100
  43.3 86.0 %all-to-all-start.1 = ((bf16[8,32,7168]{2,1,0:T(8,128)(2,1)}), bf16[8,32,7168]{2,1,0:T(8,128)(2,1)}, u32[]{:S(2)}, u32[]{:S(2)}) async-start(bf16[8,32,7168]{2,1,0:T(8,128)(2,1)} %bitcast.49), calls=%async_computation.1 | async-start | bytes 7340032 | tf_op jit(solution)/shard_map/all_to_all | solution.py:117
  129.3 85.6 %copy-start.1 = (bf16[8,896,256]{2,1,0:T(8,128)(2,1)S(1)}, bf16[8,896,256]{2,1,0:T(8,128)(2,1)}, u32[]{:S(2)}) copy-start(bf16[8,896,256]{2,1,0:T(8,128)(2,1)} %get-tuple-element.7) | copy-start | bytes 11010052
  299.8 86.3 %all-to-all-start.4 = ((bf16[8,896,256]{2,1,0:T(8,128)(2,1)}), bf16[8,896,256]{2,1,0:T(8,128)(2,1)}, u32[]{:S(2)}, u32[]{:S(2)}) async-start(bf16[8,896,256]{2,1,0:T(8,128)(2,1)} %get-tuple-element.8), calls=%async_computation.4 | async-start | bytes 7340032 | tf_op jit(solution)/shard_map/all_to_all | solution.py:90
  305.7 134.2 %reduce-scatter.2.cloned.1.call-start = ((), (), s32[]{:S(2)}) async-start(), calls=%async_computation.7 | async-start | bytes 4587520 | tf_op jit(solution)/shard_map/reduce_scatter | solution.py:124
  396.1 0.7 copy-start.5
  396.1 1.1 copy-start.6
  407.4 38.6 %copy-start.2 = (s32[32,8]{0,1:T(8,128)S(1)}, s32[32,8]{0,1:T(8,128)}, u32[]{:S(2)}) copy-start(s32[32,8]{0,1:T(8,128)} %param.22) | copy-start | bytes 3076
  439.9 27.3 %all-to-all-start.5 = ((bf16[8,32,1792]{2,1,0:T(8,128)(2,1)}), bf16[8,32,1792]{2,1,0:T(8,128)(2,1)S(1)}, u32[]{:S(2)}, u32[]{:S(2)}) async-start(bf16[8,32,1792]{2,1,0:T(8,128)(2,1)} %bitcast.51), calls=%async_computation.6 | async-start | bytes 1835008 | tf_op jit(solution)/shard_map/all_to_all | solution.py:127
Sparse Core Ops, SparseCore 0:
  396.3 43.5 reduce-scatter.1
where the time goes:
time: 488 us; the launch traced here: 483 us
  blocking collectives  196 us (40%)
  waiting for transfers between devices  172 us (35%)
  local copies, waits for them, and re-layouts  43.5 us (9%)
  matrix products  26 us (5%)
  starting transfers between devices  17.5 us (4%)
  other arithmetic  14.6 us (3%)
  between operations  14.1 us (3%)
    all_to_all x1, blocking collectives, per_device(): lax.all_to_all(jnp.take(learner_gate, learner_entry, axis=0), 'expert', s...  85.6 us
    all_to_all x1, blocking collectives, per_device(): lax.all_to_all(jnp.take(learner_up, learner_entry, axis=0), 'expert', spl...  84.9 us
    all_to_all x1, waiting for transfers between devices, per_device(): lax.all_to_all(chosen_down, 'expert', split_axis=0, concat_axis=1, tiled=...  76.1 us
    all_to_all x1, waiting for transfers between devices, per_device(): lax.all_to_all(outbound, 'expert', split_axis=0, concat_axis=0, tiled=True)  58.5 us
    reduce_scatter x1, waiting for transfers between devices, per_device(): lax.psum_scatter(partial_out.astype(jnp.bfloat16), 'tensor', scatter_dime...  19.8 us
    scatter x1, local copies, waits for them, and re-layouts, per_device(): outbound = jnp.zeros((slot_total * capacity, normed.shape[1]), jnp.bfloat...  18.3 us
    all_to_all x1, waiting for transfers between devices, per_device(): lax.all_to_all(shared, 'expert', split_axis=0, concat_axis=0, tiled=True)  17.5 us
    all_to_all x1, blocking collectives, per_device(): lax.all_to_all(latent, 'tensor', split_axis=1, concat_axis=0, tiled=True)  12.5 us
  transfers between devices with their start and end apart: 4, of which 4 were waited for; matrix products, arithmetic and copies ran while one was open for 8% of the time, Pallas kernels for 0%

commit v1 on v0

v1 whole, which is shorter than its diff:
```python
import jax
import jax.numpy as jnp
from jax import lax
from jax.sharding import PartitionSpec as P

KVL = 512


SCORE_SCALE = 192.0 ** (-0.5)
ROUTE_SCALE = 2.5
NORM_EPSILON = 1e-06


def attend(query_latent, kv_cache, cache_len):
    scores = (
        jnp.einsum("rhc,rpc->rhp", query_latent, kv_cache, preferred_element_type=jnp.float32)
        * SCORE_SCALE
    )
    allowed = (jnp.arange(kv_cache.shape[1], dtype=jnp.int32)[None, :] < cache_len[:, None])[
        :, None, :
    ]
    scores = jnp.where(allowed, scores, -1e30)
    highest = jnp.max(scores, axis=2, keepdims=True)
    lifted = jnp.where(allowed, jnp.exp(scores - highest), 0.0)
    totals = jnp.sum(lifted, axis=2, keepdims=True)
    mixed = jnp.einsum(
        "rhp,rpc->rhc",
        lifted.astype(jnp.bfloat16),
        kv_cache[:, :, :KVL],
        preferred_element_type=jnp.float32,
    )
    return (mixed / totals).astype(jnp.bfloat16)


def hand_over(learner, placement_plan, updated_list):
    expert_total, depth, width = learner.shape
    devices = lax.axis_size("expert")
    me = lax.axis_index("expert")
    held_each = placement_plan.shape[0] // devices
    entry_range = jnp.arange(expert_total, dtype=jnp.int32)
    slot_range = jnp.arange(placement_plan.shape[0], dtype=jnp.int32)

    def rows_for(device):
        blocks = []
        for held in range(held_each):
            expert = jnp.sum(jnp.where(slot_range == device * held_each + held, placement_plan, 0))
            entry = jnp.sum(jnp.where(updated_list == expert, entry_range, 0))
            blocks.append(lax.dynamic_slice_in_dim(learner, entry, 1, axis=0))
        return blocks[0] if held_each == 1 else jnp.concatenate(blocks, axis=0)

    held = jnp.zeros((held_each, depth * devices, width), learner.dtype)
    held = lax.dynamic_update_slice_in_dim(held, rows_for(me), me * depth, axis=1)
    arrivals = []
    for step in range(1, devices):
        pairs = [(i, (i + step) % devices) for i in range(devices)]
        block = lax.ppermute(rows_for((me + step) % devices), "expert", pairs)
        arrivals.append(((me - step + devices) % devices, block))
    for origin, block in arrivals:
        held = lax.dynamic_update_slice_in_dim(held, block, origin * depth, axis=1)
    return held


def per_device(
    query_latent,
    kv_cache,
    cache_len,
    value_up,
    hidden_in,
    norm_gain,
    expert_ids,
    route_weight,
    placement_plan,
    updated_list,
    learner_gate,
    learner_up,
    learner_down,
):
    held_gate = hand_over(learner_gate, placement_plan, updated_list)
    widened = hidden_in.astype(jnp.float32)
    squares = lax.psum(jnp.sum(widened * widened, axis=1, keepdims=True), "tensor")
    row_scale = lax.rsqrt(squares / (hidden_in.shape[1] * lax.axis_size("tensor")) + NORM_EPSILON)
    gained = (widened * norm_gain.astype(jnp.float32)[None, :]).astype(jnp.bfloat16)
    whole_rows = lax.all_gather(gained, "tensor", axis=1, tiled=True)
    slices = lax.all_to_all(whole_rows, "expert", split_axis=1, concat_axis=0, tiled=True)
    gate_part = jnp.einsum("rd,edh->reh", slices, learner_gate, preferred_element_type=jnp.float32)
    up_part = jnp.einsum("rd,edh->reh", slices, learner_up, preferred_element_type=jnp.float32)
    gate_sum = lax.psum_scatter(
        gate_part.astype(jnp.bfloat16), "expert", scatter_dimension=0, tiled=True
    )
    up_sum = lax.psum_scatter(
        up_part.astype(jnp.bfloat16), "expert", scatter_dimension=0, tiled=True
    )
    weights_float = route_weight.astype(jnp.float32)
    gates = ROUTE_SCALE * weights_float / jnp.sum(weights_float, axis=1, keepdims=True)
    chosen = (expert_ids[:, :, None] == updated_list[None, None, :]).astype(jnp.float32)
    share = jnp.sum(gates[:, :, None] * chosen, axis=1)
    gate_proj = gate_sum.astype(jnp.float32) * row_scale[:, :, None]
    up_proj = up_sum.astype(jnp.float32) * row_scale[:, :, None]
    activated = (jax.nn.silu(gate_proj) * up_proj * share[:, :, None]).astype(jnp.bfloat16)
    all_activated = lax.all_gather(activated, "expert", axis=0, tiled=True)
    partial_out = jnp.einsum(
        "reh,edh->rd", all_activated, learner_down, preferred_element_type=jnp.float32
    )
    returned = lax.all_to_all(
        partial_out.astype(jnp.bfloat16), "expert", split_axis=0, concat_axis=1, tiled=True
    )
    moe_out = lax.psum_scatter(returned, "tensor", scatter_dimension=1, tiled=True)
    latent = attend(query_latent, kv_cache, cache_len)
    head_rows = lax.all_to_all(latent, "tensor", split_axis=1, concat_axis=0, tiled=True)
    projected = jnp.einsum("rhc,hcv->rhv", head_rows, value_up, preferred_element_type=jnp.float32)
    attn_values = projected.astype(jnp.bfloat16).reshape(
        head_rows.shape[0], projected.shape[1] * projected.shape[2]
    )
    return (attn_values, moe_out, held_gate)


def solution(mesh):
    in_specs = (
        P(("expert", "tensor"), None, None),
        P(("expert", "tensor"), None, None),
        P(("expert", "tensor")),
        P("tensor", None, None),
        P("expert", "tensor"),
        P("tensor"),
        P("expert", None),
        P("expert", None),
        P(),
        P(),
        P(None, "expert", "tensor"),
        P(None, "expert", "tensor"),
        P(None, "expert", "tensor"),
    )
    out_specs = (P("expert", "tensor"), P("expert", "tensor"), P("expert", None, "tensor"))
    return jax.shard_map(
        per_device, mesh=mesh, in_specs=in_specs, out_specs=out_specs, check_vma=False
    )
```

time: 488 us -> 350 us (0.72)
  blocking collectives: 196 us -> 29.6 us
  waiting for transfers between devices: 172 us -> 220 us
  local copies, waits for them, and re-layouts: 43.5 us -> 18.8 us
  between operations: 14.1 us -> 28.9 us
    all_to_all x3 -> x1, blocking collectives: 183 us -> 16.6 us  [per_device(): lax.all_to_all(whole_rows, 'expert', split_axis=1, concat_axis=0, tiled=T...]
    all_to_all x3 -> x2, waiting for transfers between devices: 152 us -> 0.01 us  [the longest x1 0.01 us: per_device(): lax.all_to_all(latent, 'tensor', split_axis=1, concat_axis=0, tiled=True)]
    reduce_scatter x1 -> x3, waiting for transfers between devices: 19.8 us -> 117 us  [the longest x1 67.2 us: per_device(): lax.psum_scatter(up_part.astype(jnp.bfloat16), 'expert', scatter_dimensio...]
    ppermute x0 -> x7, waiting for transfers between devices: none -> 68.5 us  [hand_over(): block = lax.ppermute(rows_for((me + step) % devices), 'expert', pairs)]
    all_gather x0 -> x1, waiting for transfers between devices: none -> 34.2 us  [per_device(): all_activated = lax.all_gather(activated, 'expert', axis=0, tiled=True)]
    scatter x1 -> x0, local copies, waits for them, and re-layouts: 18.3 us -> none  [per_device(): outbound = jnp.zeros((slot_total * capacity, normed.shape[1]), jnp.bfloat...]
    gather x4 -> x0, local copies, waits for them, and re-layouts: 16.4 us -> none  [the longest x1 4.72 us: per_device(): jnp.take(learner_up, learner_entry, axis=0)]
    dynamic_update_slice x0 -> x7, local copies, waits for them, and re-layouts: none -> 10.7 us  [hand_over(): held = lax.dynamic_update_slice_in_dim(held, block, origin * depth, axis=1)]
  transfers between devices with their start and end apart: 4 -> 13, of which waited for: 4 -> 7; matrix products, arithmetic and copies ran while one was open for 8% -> 11% of each run, Pallas kernels for 0% -> 0%
where the time goes in v1:
time: 350 us; the launch traced here: 349 us
  waiting for transfers between devices  220 us (63%)
  blocking collectives  29.6 us (8%)
  between operations  28.9 us (8%)
  matrix products  23.8 us (7%)
  local copies, waits for them, and re-layouts  18.8 us (5%)
  starting transfers between devices  17.4 us (5%)
  other arithmetic  10.4 us (3%)
    ppermute x7, waiting for transfers between devices, hand_over(): block = lax.ppermute(rows_for((me + step) % devices), 'expert', pairs)  68.5 us
    reduce_scatter x1, waiting for transfers between devices, per_device(): lax.psum_scatter(up_part.astype(jnp.bfloat16), 'expert', scatter_dimensio...  67.2 us
    reduce_scatter x1, waiting for transfers between devices, per_device(): lax.psum_scatter(gate_part.astype(jnp.bfloat16), 'expert', scatter_dimens...  50.2 us
    all_gather x1, waiting for transfers between devices, per_device(): all_activated = lax.all_gather(activated, 'expert', axis=0, tiled=True)  34.2 us
    all_to_all x1, blocking collectives, per_device(): lax.all_to_all(whole_rows, 'expert', split_axis=1, concat_axis=0, tiled=T...  16.6 us
    dynamic_update_slice x7, local copies, waits for them, and re-layouts, hand_over(): held = lax.dynamic_update_slice_in_dim(held, block, origin * depth, axis=1)  10.7 us
    all_gather x1, blocking collectives, per_device(): whole_rows = lax.all_gather(gained, 'tensor', axis=1, tiled=True)  7.35 us
  transfers between devices with their start and end apart: 13, of which 7 were waited for; matrix products, arithmetic and copies ran while one was open for 11% of the time, Pallas kernels for 0%

profile of v1, /device:TPU:27, one launch (start us, length us, event | category | flops | bytes accessed | tf_op | source)
XLA Modules:
  0.0 349.0 jit_solution(2963852570076842286)
XLA Ops:
  9.1 7.4 %all_gather.6 = bf16[32,7168]{1,0:T(8,128)(2,1)S(1)} all-gather(bf16[32,1792]{1,0:T(8,128)(2,1)S(1)} %get-tuple-element.28), channel_id=1, replica_groups=mesh['expert'=8,'tensor'=4] {'tensor'}, dimensions={1}, use_global_device_ids=true | all-gather | bytes 573440 | tf_op jit(solution)/shard_map/all_gather | solution.py:83
  16.5 16.6 %all_to_all.56 = bf16[32,8,896]{2,0,1:T(8,128)(2,1)S(1)} all-to-all(bf16[32,8,896]{2,0,1:T(8,128)(2,1)S(1)} %bitcast.45), channel_id=1, replica_groups=mesh['expert'=8,'tensor'=4] {'expert'}, dimensions={1} | all-to-all | bytes 917504 | tf_op jit(solution)/shard_map/all_to_all | solution.py:84
  33.1 4.3 %convolution_convert_fusion.1 = bf16[256,8,256]{2,0,1:T(8,128)(2,1)} fusion(bf16[256,896,1]{1,0,2:T(8,128)(2,1)S(1)} %bitcast.47, bf16[8,896,256]{2,1,0:T(8,128)(2,1)} %param.23), kind=kOutput, calls=%fused_computation.7 | convolution fusion | flops 940048384 | bytes 5177344 | tf_op jit(solution)/shard_map/rd,edh->reh/dot_general | solution.py:85
  37.5 4.3 %convolution_convert_fusion = bf16[256,8,256]{2,0,1:T(8,128)(2,1)} fusion(bf16[256,896,1]{1,0,2:T(8,128)(2,1)S(1)} %bitcast.48, bf16[8,896,256]{2,1,0:T(8,128)(2,1)} %param.24), kind=kOutput, calls=%fused_computation.6 | convolution fusion | flops 940048384 | bytes 5177344 | tf_op jit(solution)/shard_map/rd,edh->reh/dot_general | solution.py:86
  41.9 5.6 %psum.7 = f32[32,1]{0,1:T(1,128)S(1)} all-reduce(f32[32,1]{0,1:T(1,128)S(1)} %bitcast.50), channel_id=1, replica_groups=mesh['expert'=8,'tensor'=4] {'tensor'}, use_global_device_ids=true, to_apply=%region_4.5 | all-reduce | flops 32 | bytes 256 | tf_op jit(solution)/shard_map/psum | solution.py:80
  47.6 50.2 %reduce-scatter.4.cloned.1.call-done = bf16[32,8,256]{2,0,1:T(8,128)(2,1)} async-done(((bf16[256,8,256]{2,0,1:T(8,128)(2,1)}), bf16[32,8,256]{2,0,1:T(8,128)(2,1)}) %reduce-scatter.4.cloned.1.call-update) | async-done | bytes 131088 | tf_op jit(solution)/shard_map/reduce_scatter | solution.py:87
  97.8 67.2 %reduce-scatter.6.cloned.1.call-done = bf16[32,8,256]{2,0,1:T(8,128)(2,1)} async-done(((bf16[256,8,256]{2,0,1:T(8,128)(2,1)}), bf16[32,8,256]{2,0,1:T(8,128)(2,1)}) %reduce-scatter.6.cloned.1.call-update) | async-done | bytes 131088 | tf_op jit(solution)/shard_map/reduce_scatter | solution.py:90
  167.0 5.5 %fusion.29 = (f32[8,64]{1,0:T(8,128)S(1)}, bf16[8,64,768]{2,1,0:T(8,128)(2,1)}) fusion(pred[8,768]{1,0:T(8,128)(4,1)S(1)} %iota_compare_fusion, bf16[8,64,576]{2,1,0:T(8,128)(2,1)S(1)} %copy-done.8, bf16[8,768,576]{1,2,0:T(8,128)(2,1)} %param.14), kind=kOutput, calls=%fused_computation.75 | convolution fusion | flops 455344896 | bytes 8462336 | tf_op jit(solution)/shard_map/sub | solution.py:24
  172.6 34.2 %all-gather.2.cloned.1.call-done = bf16[256,8,256]{2,0,1:T(8,128)(2,1)} async-done(((bf16[32,8,256]{2,0,1:T(8,128)(2,1)}), bf16[256,8,256]{2,0,1:T(8,128)(2,1)}) %all-gather.2.cloned.1.call-update) | async-done | bytes 1048592 | tf_op jit(solution)/shard_map/all_gather | solution.py:100
  206.7 4.4 %fusion.4 = bf16[256,896]{1,0:T(8,128)(2,1)} fusion(bf16[256,8,256]{2,0,1:T(8,128)(2,1)} %all-gather.2.cloned.1.call-done, bf16[8,896,256]{2,1,0:T(8,128)(2,1)} %param.25), kind=kOutput, calls=%fused_computation.9 | convolution fusion | flops 939753472 | bytes 5177344 | tf_op jit(solution)/shard_map/reh,edh->rd/dot_general | solution.py:101
  211.1 6.6 %all-to-all-start.2 = ((bf16[8,32,896]{2,1,0:T(8,128)(2,1)}), bf16[8,32,896]{2,1,0:T(8,128)(2,1)S(1)}, u32[]{:S(2)}, u32[]{:S(2)}) async-start(bf16[8,32,896]{2,1,0:T(8,128)(2,1)} %bitcast.12), calls=%async_computation.4 | async-start | bytes 917504 | tf_op jit(solution)/shard_map/all_to_all | solution.py:104
  218.5 5.8 %fusion.28 = (s32[]{:T(128)}, s32[]{:T(128)}, s32[]{:T(128)}, s32[]{:T(128)}, s32[]{:T(128)}, /*index=5*/s32[]{:T(128)}, s32[]{:T(128)}, s32[]{:T(128)}) fusion(s32[8]{0:T(128)S(1)} %copy-done.5, s32[]{:T(128)} %get-tuple-element.11, s32[]{:T(128)} %get-tuple-element.12, s32[]{:T(128)} %get-tuple-element.13, s32[]{:T(128)} %get-tuple-element.14, ...), kind=kLoop, calls=%fused_computation.73 | loop fusion | flops 184 | bytes 96 | tf_op jit(solution)/shard_map/reduce_sum | solution.py:47
  234.3 4.9 %divide_convert_fusion = bf16[8,64,512]{2,1,0:T(8,128)(2,1)S(1)} fusion(bf16[8,768,576]{1,2,0:T(8,128)(2,1)} %param.14, bf16[8,64,768]{2,1,0:T(8,128)(2,1)S(1)} %copy-done.9, f32[8,64]{1,0:T(8,128)S(1)} %get-tuple-element.29), kind=kOutput, calls=%fused_computation.12 | convolution fusion | flops 403177472 | bytes 7604224 | tf_op jit(solution)/shard_map/rhp,rpc->rhc/dot_general | solution.py:26
  245.2 5.4 %all-to-all-start = ((bf16[8,64,512]{2,0,1:T(8,128)(2,1)}), bf16[8,64,512]{2,0,1:T(8,128)(2,1)S(1)}, u32[]{:S(2)}, u32[]{:S(2)}) async-start(bf16[8,64,512]{2,0,1:T(8,128)(2,1)} %copy.38), calls=%async_computation | async-start | bytes 1048576 | tf_op jit(solution)/shard_map/all_to_all | solution.py:109
  254.2 1.8 copy-done.2
  263.0 5.4 %collective-permute-done = bf16[1,896,256]{2,1,0:T(8,128)(2,1)} collective-permute-done((bf16[1,896,256]{2,1,0:T(8,128)(2,1)}, bf16[1,896,256]{2,1,0:T(8,128)(2,1)}, u32[]{:S(2)}, u32[]{:S(2)}) %collective-permute-start) | collective-permute-done | bytes 458784 | tf_op jit(solution)/shard_map/ppermute | solution.py:56
  268.7 1.8 constant_dynamic-update-slice_fusion.5
  270.5 7.7 %collective-permute-done.1 = bf16[1,896,256]{2,1,0:T(8,128)(2,1)} collective-permute-done((bf16[1,896,256]{2,1,0:T(8,128)(2,1)}, bf16[1,896,256]{2,1,0:T(8,128)(2,1)}, u32[]{:S(2)}, u32[]{:S(2)}) %collective-permute-start.1) | collective-permute-done | bytes 458784 | tf_op jit(solution)/shard_map/ppermute | solution.py:56
  278.3 1.8 constant_dynamic-update-slice_fusion.4
  280.1 6.1 %collective-permute-done.2 = bf16[1,896,256]{2,1,0:T(8,128)(2,1)} collective-permute-done((bf16[1,896,256]{2,1,0:T(8,128)(2,1)}, bf16[1,896,256]{2,1,0:T(8,128)(2,1)}, u32[]{:S(2)}, u32[]{:S(2)}) %collective-permute-start.2) | collective-permute-done | bytes 458784 | tf_op jit(solution)/shard_map/ppermute | solution.py:56
  286.2 1.8 constant_dynamic-update-slice_fusion.3
  288.0 49.2 %collective-permute-done.3 = bf16[1,896,256]{2,1,0:T(8,128)(2,1)} collective-permute-done((bf16[1,896,256]{2,1,0:T(8,128)(2,1)}, bf16[1,896,256]{2,1,0:T(8,128)(2,1)}, u32[]{:S(2)}, u32[]{:S(2)}) %collective-permute-start.3) | collective-permute-done | bytes 458784 | tf_op jit(solution)/shard_map/ppermute | solution.py:56
  337.2 1.8 constant_dynamic-update-slice_fusion.2
  339.0 1.8 constant_dynamic-update-slice_fusion.1
  (58 shorter events, 18.4 us)
Async XLA Ops:
  7.2 254.8 %copy-start = (bf16[16,512,128]{2,1,0:T(8,128)(2,1)S(1)}, bf16[16,512,128]{2,1,0:T(8,128)(2,1)}, u32[]{:S(2)}) copy-start(bf16[16,512,128]{2,1,0:T(8,128)(2,1)} %param.16) | copy-start | bytes 6291460
  7.2 90.6 %reduce-scatter.4.cloned.1.call-start = ((), (), s32[]{:S(2)}) async-start(), calls=%async_computation.6 | async-start | bytes 1179648 | tf_op jit(solution)/shard_map/reduce_scatter | solution.py:87
  37.4 10.1 %copy-start.3 = (s32[32,8]{0,1:T(8,128)S(1)}, s32[32,8]{0,1:T(8,128)}, u32[]{:S(2)}) copy-start(s32[32,8]{0,1:T(8,128)} %param.20) | copy-start | bytes 3076
  37.4 10.1 %copy-start.4 = (s32[32,8]{0,1:T(8,128)S(1)}, s32[32,8]{0,1:T(8,128)}, u32[]{:S(2)}) copy-start(s32[32,8]{0,1:T(8,128)} %param.19) | copy-start | bytes 3076
  37.4 10.1 %copy-start.5 = (s32[8]{0:T(128)S(1)}, s32[8]{0:T(128)}, u32[]{:S(2)}) copy-start(s32[8]{0:T(128)} %param.22) | copy-start | bytes 100
  37.4 129.5 %copy-start.7 = (s32[8]{0:T(128)S(1)}, s32[8]{0:T(128)}, u32[]{:S(2)}) copy-start(s32[8]{0:T(128)} %param.15) | copy-start | bytes 100
  37.4 129.6 %copy-start.8 = (bf16[8,64,576]{2,1,0:T(8,128)(2,1)S(1)}, bf16[8,64,576]{2,1,0:T(8,128)(2,1)}, u32[]{:S(2)}) copy-start(bf16[8,64,576]{2,1,0:T(8,128)(2,1)} %param.13) | copy-start | bytes 1769476
  37.5 127.6 %reduce-scatter.6.cloned.1.call-start = ((), (), s32[]{:S(2)}) async-start(), calls=%async_computation.7 | async-start | bytes 1179648 | tf_op jit(solution)/shard_map/reduce_scatter | solution.py:90
  41.8 164.9 %all-gather.2.cloned.1.call-start = ((), (), s32[]{:S(2)}) async-start(), calls=%async_computation.8 | async-start | bytes 1179648 | tf_op jit(solution)/shard_map/all_gather | solution.py:100
  172.6 45.2 %copy-start.6 = (s32[8]{0:T(128)S(1)}, s32[8]{0:T(128)}, u32[]{:S(2)}) copy-start(s32[8]{0:T(128)} %param.21) | copy-start | bytes 100
  172.6 61.7 %copy-start.9 = (bf16[8,64,768]{2,1,0:T(8,128)(2,1)S(1)}, bf16[8,64,768]{2,1,0:T(8,128)(2,1)}, u32[]{:S(2)}) copy-start(bf16[8,64,768]{2,1,0:T(8,128)(2,1)} %get-tuple-element.30) | copy-start | bytes 2359300
  211.1 34.1 %all-to-all-start.2 = ((bf16[8,32,896]{2,1,0:T(8,128)(2,1)}), bf16[8,32,896]{2,1,0:T(8,128)(2,1)S(1)}, u32[]{:S(2)}, u32[]{:S(2)}) async-start(bf16[8,32,896]{2,1,0:T(8,128)(2,1)} %bitcast.12), calls=%async_computation.4 | async-start | bytes 917504 | tf_op jit(solution)/shard_map/all_to_all | solution.py:104
  245.2 16.7 %all-to-all-start = ((bf16[8,64,512]{2,0,1:T(8,128)(2,1)}), bf16[8,64,512]{2,0,1:T(8,128)(2,1)S(1)}, u32[]{:S(2)}, u32[]{:S(2)}) async-start(bf16[8,64,512]{2,0,1:T(8,128)(2,1)} %copy.38), calls=%async_computation | async-start | bytes 1048576 | tf_op jit(solution)/shard_map/all_to_all | solution.py:109
  250.6 91.9 %reduce-scatter.8.cloned.1.call-start = ((), (), s32[]{:S(2)}) async-start(), calls=%async_computation.9 | async-start | bytes 573440 | tf_op jit(solution)/shard_map/reduce_scatter | solution.py:107
  250.6 2.0 copy-start.1
  254.2 1.8 copy-start.2
  256.0 12.4 %collective-permute-start = (bf16[1,896,256]{2,1,0:T(8,128)(2,1)}, bf16[1,896,256]{2,1,0:T(8,128)(2,1)}, u32[]{:S(2)}, u32[]{:S(2)}) collective-permute-start(bf16[1,896,256]{2,1,0:T(8,128)(2,1)} %get-tuple-element.24), channel_id=1, source_target_pairs={{0,4},{4,8},{8,12},{12,16},{16,20},{20,24},{24,28},{28,0},{1,5},{5... | collective-permute-start | bytes 1376264 | tf_op jit(solution)/shard_map/ppermute | solution.py:56
  256.0 22.2 %collective-permute-start.1 = (bf16[1,896,256]{2,1,0:T(8,128)(2,1)}, bf16[1,896,256]{2,1,0:T(8,128)(2,1)}, u32[]{:S(2)}, u32[]{:S(2)}) collective-permute-start(bf16[1,896,256]{2,1,0:T(8,128)(2,1)} %get-tuple-element.23), channel_id=1, source_target_pairs={{0,8},{4,12},{8,16},{12,20},{16,24},{20,28},{24,0},{28,4},{1,9},{5... | collective-permute-start | bytes 1376264 | tf_op jit(solution)/shard_map/ppermute | solution.py:56
  257.5 28.7 %collective-permute-start.2 = (bf16[1,896,256]{2,1,0:T(8,128)(2,1)}, bf16[1,896,256]{2,1,0:T(8,128)(2,1)}, u32[]{:S(2)}, u32[]{:S(2)}) collective-permute-start(bf16[1,896,256]{2,1,0:T(8,128)(2,1)} %get-tuple-element.22), channel_id=1, source_target_pairs={{0,12},{4,16},{8,20},{12,24},{16,28},{20,0},{24,4},{28,8},{1,13},{... | collective-permute-start | bytes 1376264 | tf_op jit(solution)/shard_map/ppermute | solution.py:56
  258.7 78.5 %collective-permute-start.3 = (bf16[1,896,256]{2,1,0:T(8,128)(2,1)}, bf16[1,896,256]{2,1,0:T(8,128)(2,1)}, u32[]{:S(2)}, u32[]{:S(2)}) collective-permute-start(bf16[1,896,256]{2,1,0:T(8,128)(2,1)} %get-tuple-element.21), channel_id=1, source_target_pairs={{0,16},{4,20},{8,24},{12,28},{16,0},{20,4},{24,8},{28,12},{1,17},{... | collective-permute-start | bytes 1376264 | tf_op jit(solution)/shard_map/ppermute | solution.py:56
  259.8 79.2 %collective-permute-start.4 = (bf16[1,896,256]{2,1,0:T(8,128)(2,1)}, bf16[1,896,256]{2,1,0:T(8,128)(2,1)}, u32[]{:S(2)}, u32[]{:S(2)}) collective-permute-start(bf16[1,896,256]{2,1,0:T(8,128)(2,1)} %get-tuple-element.20), channel_id=1, source_target_pairs={{0,20},{4,24},{8,28},{12,0},{16,4},{20,8},{24,12},{28,16},{1,21},{... | collective-permute-start | bytes 1376264 | tf_op jit(solution)/shard_map/ppermute | solution.py:56
  268.4 72.4 %collective-permute-start.5 = (bf16[1,896,256]{2,1,0:T(8,128)(2,1)}, bf16[1,896,256]{2,1,0:T(8,128)(2,1)S(1)}, u32[]{:S(2)}, u32[]{:S(2)}) collective-permute-start(bf16[1,896,256]{2,1,0:T(8,128)(2,1)} %get-tuple-element.26), channel_id=1, source_target_pairs={{0,24},{4,28},{8,0},{12,4},{16,8},{20,12},{24,16},{28,20},{1,25},{... | collective-permute-start | bytes 1376264 | tf_op jit(solution)/shard_map/ppermute | solution.py:56
  278.3 63.4 %collective-permute-start.6 = (bf16[1,896,256]{2,1,0:T(8,128)(2,1)S(1)}, bf16[1,896,256]{2,1,0:T(8,128)(2,1)S(1)}, u32[]{:S(2)}, u32[]{:S(2)}) collective-permute-start(bf16[1,896,256]{2,1,0:T(8,128)(2,1)S(1)} %get-tuple-element.19), channel_id=1, source_target_pairs={{0,28},{4,0},{8,4},{12,8},{16,12},{20,16},{24,20},{28,24},{1,29},{... | collective-permute-start | bytes 1376264 | tf_op jit(solution)/shard_map/ppermute | solution.py:56
Sparse Core Ops, SparseCore 0:
  37.5 60.2 reduce-scatter.3
  102.2 62.8 reduce-scatter.5
  167.8 38.8 all-gather.1
  262.0 23.3 reduce-scatter.7

commit v2 on v1

v2 whole, which is shorter than its diff:
```python
import functools

import jax
import jax.numpy as jnp
from jax import lax
from jax.experimental import pallas as pl
from jax.experimental.pallas import tpu as pltpu
from jax.sharding import PartitionSpec as P

KVL = 512


SCORE_SCALE = 192.0 ** (-0.5)
ROUTE_SCALE = 2.5
NORM_EPSILON = 1e-06


def attend(query_latent, kv_cache, cache_len):
    scores = (
        jnp.einsum("rhc,rpc->rhp", query_latent, kv_cache, preferred_element_type=jnp.float32)
        * SCORE_SCALE
    )
    allowed = (jnp.arange(kv_cache.shape[1], dtype=jnp.int32)[None, :] < cache_len[:, None])[
        :, None, :
    ]
    scores = jnp.where(allowed, scores, -1e30)
    highest = jnp.max(scores, axis=2, keepdims=True)
    lifted = jnp.where(allowed, jnp.exp(scores - highest), 0.0)
    totals = jnp.sum(lifted, axis=2, keepdims=True)
    mixed = jnp.einsum(
        "rhp,rpc->rhc",
        lifted.astype(jnp.bfloat16),
        kv_cache[:, :, :KVL],
        preferred_element_type=jnp.float32,
    )
    return (mixed / totals).astype(jnp.bfloat16)


def pick_entries(learner, entries):
    depth, width = learner.shape[1:]

    def copy(entries_ref, in_ref, out_ref):
        out_ref[...] = in_ref[...]

    return pl.pallas_call(
        copy,
        grid_spec=pltpu.PrefetchScalarGridSpec(
            num_scalar_prefetch=1,
            grid=(entries.shape[0],),
            in_specs=[pl.BlockSpec((1, depth, width), lambda s, e: (e[s], 0, 0))],
            out_specs=pl.BlockSpec((1, depth, width), lambda s, e: (s, 0, 0)),
        ),
        out_shape=jax.ShapeDtypeStruct((entries.shape[0], depth, width), learner.dtype),
    )(entries, learner)


def moe_kernel(
    devices,
    lanes,
    x_ref,
    square_ref,
    share_ref,
    chosen_ref,
    gate_hbm,
    up_hbm,
    down_hbm,
    out_ref,
    held_ref,
    rows,
    squares,
    gate_w,
    up_w,
    down_w,
    parts,
    came,
    acts,
    total,
    leaving,
    back,
    local_sem,
    row_send,
    row_recv,
    square_send,
    square_recv,
    part_send,
    part_recv,
    act_send,
    act_recv,
    back_send,
    back_recv,
    held_send,
    held_recv,
):
    i, t = lax.axis_index("expert"), lax.axis_index("tensor")
    per = devices // lanes
    entries, depth, width = gate_w.shape
    row_count = x_ref.shape[1]
    whole = devices * lanes
    me = i * lanes + t

    def remote(src, dst, send, recv, expert, tensor):
        return pltpu.make_async_remote_copy(
            src_ref=src,
            dst_ref=dst,
            send_sem=send,
            recv_sem=recv,
            device_id=(expert, tensor),
            device_id_type=pl.DeviceIdType.MESH,
        )

    def each(first, last, body):
        lax.fori_loop(first, last, lambda k, c: (body(k), c)[1], 0)

    loads = [
        pltpu.make_async_copy(gate_hbm, gate_w, local_sem.at[0]),
        pltpu.make_async_copy(up_hbm, up_w, local_sem.at[1]),
        pltpu.make_async_copy(down_hbm, down_w, local_sem.at[2]),
    ]
    for load in loads:
        load.start()
    own = pltpu.make_async_copy(chosen_ref.at[i], held_ref.at[i], local_sem.at[3])
    own.start()

    barrier = pltpu.get_barrier_semaphore()

    def greet(k):
        other = lax.rem(me + k, whole)
        pl.semaphore_signal(
            barrier,
            inc=1,
            device_id=(other // lanes, lax.rem(other, lanes)),
            device_id_type=pl.DeviceIdType.MESH,
        )

    each(1, whole, greet)
    pl.semaphore_wait(barrier, whole - 1)

    def row_copy(p, k):
        to = lax.rem(t + k, lanes)
        return remote(
            x_ref.at[p], rows.at[i], row_send.at[p * lanes + k], row_recv.at[i], t * per + p, to
        )

    for p in range(per):
        each(1, lanes, lambda k, p=p: row_copy(p, k).start())
        pl.when(t * per + p != i)(lambda p=p: row_copy(p, 0).start())

    def square_copy(k):
        to = lax.rem(t + k, lanes)
        return remote(square_ref, squares.at[t], square_send.at[k], square_recv.at[t], i, to)

    each(1, lanes, lambda k: square_copy(k).start())

    def held_copy(k):
        to = lax.rem(i + k, devices)
        return remote(
            chosen_ref.at[to], held_ref.at[i], held_send.at[k], held_recv.at[i], to, t
        )

    each(1, devices, lambda k: held_copy(k).start())

    home = i // per

    @pl.when(home == t)
    def _():
        rows[i] = x_ref[lax.rem(i, per)]

    squares[t] = square_ref[...]

    def row_arrival(k):
        origin = lax.rem(i + k, devices)
        remote(
            x_ref.at[0], rows.at[origin], row_send.at[0], row_recv.at[origin], origin, home
        ).wait_recv()

    each(1, devices, row_arrival)
    pl.when(home != t)(lambda: row_arrival(0))
    loads[0].wait()
    loads[1].wait()

    def project(e):
        arrived = rows[...].reshape(devices * row_count, depth)
        for which, weight in enumerate((gate_w, up_w)):
            product = jnp.dot(arrived, weight[e], preferred_element_type=jnp.float32)
            parts[:, which, e] = product.astype(jnp.bfloat16).reshape(devices, row_count, width)

    each(0, entries, project)

    def part_copy(k):
        to = lax.rem(i + k, devices)
        return remote(parts.at[to], came.at[i], part_send.at[k], part_recv.at[i], to, t)

    each(1, devices, lambda k: part_copy(k).start())
    came[i] = parts[i]

    def square_arrival(k):
        origin = lax.rem(t + k, lanes)
        remote(
            square_ref, squares.at[origin], square_send.at[0], square_recv.at[origin], i, origin
        ).wait_recv()

    each(1, lanes, square_arrival)
    features = depth * devices
    row_scale = lax.rsqrt(jnp.sum(squares[...], axis=0) / features + NORM_EPSILON)[:, :1]

    def part_arrival(k):
        origin = lax.rem(i + k, devices)
        remote(
            parts.at[0], came.at[origin], part_send.at[0], part_recv.at[origin], origin, t
        ).wait_recv()

    each(1, devices, part_arrival)

    def activate(e):
        gate = jnp.sum(came[:, 0, e].astype(jnp.float32), axis=0) * row_scale
        up = jnp.sum(came[:, 1, e].astype(jnp.float32), axis=0) * row_scale
        silu = gate / (1.0 + jnp.exp(-gate))
        acts[i, e] = (silu * up * share_ref[e]).astype(jnp.bfloat16)

    each(0, entries, activate)

    def act_copy(k):
        to = lax.rem(i + k, devices)
        return remote(acts.at[i], acts.at[i], act_send.at[k], act_recv.at[i], to, t)

    each(1, devices, lambda k: act_copy(k).start())
    loads[2].wait()

    def act_arrival(k):
        origin = lax.rem(i + k, devices)
        remote(
            acts.at[i], acts.at[origin], act_send.at[0], act_recv.at[origin], origin, t
        ).wait_recv()

    each(1, devices, act_arrival)
    total[...] = jnp.zeros_like(total)

    def lower(e):
        total[...] += lax.dot_general(
            acts[:, e].reshape(devices * row_count, width),
            down_w[e],
            (((1,), (1,)), ((), ())),
            preferred_element_type=jnp.float32,
        )

    each(0, entries, lower)
    leaving[...] = total[...].astype(jnp.bfloat16).reshape(devices, row_count, depth)

    place = lax.rem(i, per) * lanes + t

    def back_copy(k):
        to = lax.rem(i + k, devices)
        return remote(leaving.at[to], back.at[place], back_send.at[k], back_recv.at[place], to, home)

    each(1, devices, lambda k: back_copy(k).start())
    pl.when(home != t)(lambda: back_copy(0).start())

    @pl.when(home == t)
    def _():
        back[place] = leaving[i]

    def back_arrival(p, k):
        lane = lax.rem(t + k, lanes)
        slot = p * lanes + lane
        remote(
            leaving.at[0], back.at[slot], back_send.at[0], back_recv.at[slot], t * per + p, lane
        ).wait_recv()

    for p in range(per):
        each(1, lanes, lambda k, p=p: back_arrival(p, k))
        pl.when(t * per + p != i)(lambda p=p: back_arrival(p, 0))
    for p in range(per):
        summed = jnp.zeros((row_count, depth), jnp.float32)
        for lane in range(lanes):
            summed += back[p * lanes + lane].astype(jnp.float32)
        out_ref[p] = summed.astype(jnp.bfloat16)

    for p in range(per):
        each(1, lanes, lambda k, p=p: row_copy(p, k).wait_send())
        pl.when(t * per + p != i)(lambda p=p: row_copy(p, 0).wait_send())
    each(1, lanes, lambda k: square_copy(k).wait_send())
    each(1, devices, lambda k: part_copy(k).wait_send())
    each(1, devices, lambda k: act_copy(k).wait_send())
    each(1, devices, lambda k: back_copy(k).wait_send())
    pl.when(home != t)(lambda: back_copy(0).wait_send())

    def held_arrival(k):
        origin = lax.rem(i + k, devices)
        remote(
            chosen_ref.at[0], held_ref.at[origin], held_send.at[0], held_recv.at[origin], origin, t
        ).wait_recv()

    each(1, devices, held_arrival)
    each(1, devices, lambda k: held_copy(k).wait_send())
    own.wait()


def moe(x, square, share, chosen, gate, up, down, devices, lanes):
    entries, depth, width = gate.shape
    per, row_count = x.shape[:2]
    held_each = chosen.shape[1]
    vmem = pl.BlockSpec(memory_space=pltpu.VMEM)
    anywhere = pl.BlockSpec(memory_space=pl.ANY)
    bf16 = jnp.bfloat16
    dma = pltpu.SemaphoreType.DMA
    return pl.pallas_call(
        functools.partial(moe_kernel, devices, lanes),
        out_shape=(
            jax.ShapeDtypeStruct((per, row_count, depth), bf16),
            jax.ShapeDtypeStruct((devices, held_each, depth, width), bf16),
        ),
        in_specs=[vmem, vmem, vmem, anywhere, anywhere, anywhere, anywhere],
        out_specs=(vmem, anywhere),
        scratch_shapes=[
            pltpu.VMEM((devices, row_count, depth), bf16),
            pltpu.VMEM((lanes,) + square.shape, jnp.float32),
            pltpu.VMEM(gate.shape, bf16),
            pltpu.VMEM(up.shape, bf16),
            pltpu.VMEM(down.shape, bf16),
            pltpu.VMEM((devices, 2, entries, row_count, width), bf16),
            pltpu.VMEM((devices, 2, entries, row_count, width), bf16),
            pltpu.VMEM((devices, entries, row_count, width), bf16),
            pltpu.VMEM((devices * row_count, depth), jnp.float32),
            pltpu.VMEM((devices, row_count, depth), bf16),
            pltpu.VMEM((per * lanes, row_count, depth), bf16),
            dma((4,)),
            dma((per * lanes,)),
            dma((devices,)),
            dma((lanes,)),
            dma((lanes,)),
            dma((devices,)),
            dma((devices,)),
            dma((devices,)),
            dma((devices,)),
            dma((devices,)),
            dma((per * lanes,)),
            dma((devices,)),
            dma((devices,)),
        ],
        compiler_params=pltpu.CompilerParams(
            collective_id=0, has_side_effects=True, vmem_limit_bytes=60 * 1024 * 1024
        ),
        cost_estimate=pl.CostEstimate(
            flops=6 * devices * row_count * entries * depth * width,
            bytes_accessed=10 * entries * depth * width,
            transcendentals=row_count * entries * width,
        ),
    )(x, square, share, chosen, gate, up, down)


def per_device(
    query_latent,
    kv_cache,
    cache_len,
    value_up,
    hidden_in,
    norm_gain,
    expert_ids,
    route_weight,
    placement_plan,
    updated_list,
    learner_gate,
    learner_up,
    learner_down,
):
    expert_total, depth, width = learner_gate.shape
    devices, lanes = lax.axis_size("expert"), lax.axis_size("tensor")
    per = devices // lanes
    row_count = hidden_in.shape[0]
    slot_total = placement_plan.shape[0]
    held_each = slot_total // devices
    entry_range = jnp.arange(expert_total, dtype=jnp.int32)
    learner_entry = jnp.sum(
        entry_range[None, :] * (updated_list[None, :] == placement_plan[:, None]).astype(jnp.int32),
        axis=1,
    )
    chosen_gate = pick_entries(learner_gate, learner_entry).reshape(
        devices, held_each, depth, width
    )
    widened = hidden_in.astype(jnp.float32)
    square = jnp.broadcast_to(jnp.sum(widened * widened, axis=1, keepdims=True), (row_count, 128))
    gained = (widened * norm_gain.astype(jnp.float32)[None, :]).astype(jnp.bfloat16)
    gained = jnp.swapaxes(gained.reshape(row_count, per, depth), 0, 1)
    weights_float = route_weight.astype(jnp.float32)
    gates = ROUTE_SCALE * weights_float / jnp.sum(weights_float, axis=1, keepdims=True)
    named = (expert_ids[None, :, :] == updated_list[:, None, None]).astype(jnp.float32)
    share = jnp.sum(gates[None, :, :] * named, axis=2)
    share = jnp.broadcast_to(share[:, :, None], (expert_total, row_count, width))
    moe_parts, held = moe(
        gained, square, share, chosen_gate, learner_gate, learner_up, learner_down, devices, lanes
    )
    moe_out = jnp.swapaxes(moe_parts, 0, 1).reshape(row_count, per * depth)
    held_gate = jnp.swapaxes(held, 0, 1).reshape(held_each, devices * depth, width)
    latent = attend(query_latent, kv_cache, cache_len)
    head_rows = lax.all_to_all(latent, "tensor", split_axis=1, concat_axis=0, tiled=True)
    projected = jnp.einsum("rhc,hcv->rhv", head_rows, value_up, preferred_element_type=jnp.float32)
    attn_values = projected.astype(jnp.bfloat16).reshape(
        head_rows.shape[0], projected.shape[1] * projected.shape[2]
    )
    return (attn_values, moe_out, held_gate)


def solution(mesh):
    in_specs = (
        P(("expert", "tensor"), None, None),
        P(("expert", "tensor"), None, None),
        P(("expert", "tensor")),
        P("tensor", None, None),
        P("expert", "tensor"),
        P("tensor"),
        P("expert", None),
        P("expert", None),
        P(),
        P(),
        P(None, "expert", "tensor"),
        P(None, "expert", "tensor"),
        P(None, "expert", "tensor"),
    )
    out_specs = (P("expert", "tensor"), P("expert", "tensor"), P("expert", None, "tensor"))
    return jax.shard_map(
        per_device, mesh=mesh, in_specs=in_specs, out_specs=out_specs, check_vma=False
    )
```

time: 350 us -> 236 us (0.67)
  waiting for transfers between devices: 220 us -> 0.01 us
  Pallas kernels: 0 us -> 206 us
  blocking collectives: 29.6 us -> 0 us
  between operations: 28.9 us -> 0.73 us
  matrix products: 23.8 us -> 10.2 us
  starting transfers between devices: 17.4 us -> 4.11 us
  local copies, waits for them, and re-layouts: 18.8 us -> 9.61 us
  other arithmetic: 10.4 us -> 1.84 us
    pallas_call x0 -> x2, Pallas kernels: none -> 206 us  [the longest x1 199 us: moe(): pl.pallas_call(functools.partial(moe_kernel, devices, lanes), out_shape=(...]
    reduce_scatter x3 -> x0, waiting for transfers between devices: 117 us -> none  [the longest x1 67.2 us: per_device(): lax.psum_scatter(up_part.astype(jnp.bfloat16), 'expert', scatter_dimensio...]
    ppermute x7 -> x0, waiting for transfers between devices: 68.5 us -> none  [hand_over(): block = lax.ppermute(rows_for((me + step) % devices), 'expert', pairs)]
    all_gather x1 -> x0, waiting for transfers between devices: 34.2 us -> none  [per_device(): all_activated = lax.all_gather(activated, 'expert', axis=0, tiled=True)]
    all_to_all x1 -> x0, blocking collectives: 16.6 us -> none  [per_device(): lax.all_to_all(whole_rows, 'expert', split_axis=1, concat_axis=0, tiled=T...]
    dot_general x3 -> x0, matrix products: 13 us -> none  [the longest x1 4.42 us: per_device(): jnp.einsum('reh,edh->rd', all_activated, learner_down, preferred_element_...]
    dynamic_update_slice x7 -> x0, local copies, waits for them, and re-layouts: 10.7 us -> none  [hand_over(): held = lax.dynamic_update_slice_in_dim(held, block, origin * depth, axis=1)]
    all_gather x1 -> x0, blocking collectives: 7.35 us -> none  [per_device(): whole_rows = lax.all_gather(gained, 'tensor', axis=1, tiled=True)]
  transfers between devices with their start and end apart: 13 -> 1, of which waited for: 7 -> 0; matrix products, arithmetic and copies ran while one was open for 11% -> 2% of each run, Pallas kernels for 0% -> 89%
where the time goes in v2:
time: 236 us; the launch traced here: 233 us
  Pallas kernels  206 us (87%)
  matrix products  10.2 us (4%)
  local copies, waits for them, and re-layouts  9.61 us (4%)
  starting transfers between devices  4.11 us (2%)
    pallas_call x1, Pallas kernels, moe(): pl.pallas_call(functools.partial(moe_kernel, devices, lanes), out_shape=(...  199 us
    pallas_call x1, Pallas kernels, pick_entries(): pl.pallas_call(copy, grid_spec=pltpu.PrefetchScalarGridSpec(num_scalar_pr...  7.16 us
    sub x1, matrix products, attend(): lifted = jnp.where(allowed, jnp.exp(scores - highest), 0.0)  4.89 us
    dot_general x1, matrix products, attend(): jnp.einsum('rhp,rpc->rhc', lifted.astype(jnp.bfloat16), kv_cache[:, :, :K...  4.85 us
  transfers between devices with their start and end apart: 1, of which 0 were waited for; matrix products, arithmetic and copies ran while one was open for 2% of the time, Pallas kernels for 89%

profile of v2, /device:TPU:27, one launch (start us, length us, event | category | flops | bytes accessed | tf_op | source)
XLA Modules:
  0.0 232.7 jit_solution(1760208699938613722)
XLA Ops:
  0.6 0.0 copy-start
  0.6 0.9 iota_compare_fusion
  1.5 4.9 %fusion.12 = (f32[8,64]{1,0:T(8,128)S(1)}, bf16[8,64,768]{2,1,0:T(8,128)(2,1)S(1)}) fusion(pred[8,768]{1,0:T(8,128)(4,1)S(1)} %iota_compare_fusion, bf16[8,64,576]{2,1,0:T(8,128)(2,1)} %param.13, bf16[8,768,576]{1,2,0:T(8,128)(2,1)} %param.14), kind=kOutput, calls=%fused_computation.23 | convolution fusion | flops 455344896 | bytes 8462336 | tf_op jit(solution)/shard_map/sub | solution.py:28
  6.4 0.0 copy-start.3
  6.4 0.0 copy-start.2
  6.4 0.0 copy-start.1
  6.4 0.0 copy-start.5
  6.5 0.0 copy-start.6
  6.5 4.9 %divide_convert_fusion = bf16[8,64,512]{2,1,0:T(8,128)(2,1)S(1)} fusion(bf16[8,768,576]{1,2,0:T(8,128)(2,1)} %param.14, bf16[8,64,768]{2,1,0:T(8,128)(2,1)S(1)} %get-tuple-element.10, f32[8,64]{1,0:T(8,128)S(1)} %get-tuple-element.9), kind=kOutput, calls=%fused_computation.8 | convolution fusion | flops 403177472 | bytes 7604224 | tf_op jit(solution)/shard_map/rhp,rpc->rhc/dot_general | solution.py:30
  11.3 1.1 copy.36
  12.4 4.1 %all-to-all-start = ((bf16[8,64,512]{2,0,1:T(8,128)(2,1)}), bf16[8,64,512]{2,0,1:T(8,128)(2,1)S(1)}, u32[]{:S(2)}, u32[]{:S(2)}) async-start(bf16[8,64,512]{2,0,1:T(8,128)(2,1)} %copy.36), calls=%async_computation | async-start | bytes 1048576 | tf_op jit(solution)/shard_map/all_to_all | solution.py:395
  16.6 0.1 fusion.11
  16.8 0.7 select_reduce_fusion.1.entries_ref
  17.5 0.7 copy.52
  18.1 7.2 %shard_map.148 = bf16[8,896,256]{2,1,0:T(8,128)(2,1)} custom-call(s32[8]{0:T(128)} %select_reduce_fusion.1.entries_ref, bf16[8,896,256]{2,1,0:T(8,128)(2,1)} %gate_hbm.1), custom_call_target="tpu_custom_call" | custom-call | tf_op jit(solution)/shard_map/pallas_call | solution.py:45
  25.3 0.1 select_reduce_fusion
  25.4 0.7 broadcast_in_dim.21.square_ref
  26.0 0.8 broadcast_in_dim.22.share_ref
  26.8 199.1 %shard_map.149 = (bf16[2,32,896]{2,1,0:T(8,128)(2,1)}, bf16[8,1,896,256]{3,2,1,0:T(8,128)(2,1)}) custom-call(bf16[2,32,896]{2,1,0:T(8,128)(2,1)} %bitcast.31, f32[32,128]{1,0:T(8,128)} %broadcast_in_dim.21.square_ref, f32[8,32,256]{2,1,0:T(8,128)} %broadcast_in_dim.22.share_ref, bf16[8,1,896,256]{3,2,1,0:T(8,128)(2,1)} %bitcast.28, ...), custom_call_target="tpu_custom_call" | custom-call | flops 2818572288 | bytes 18350080 | tf_op jit(solution)/shard_map/pallas_call | solution.py:306
  225.9 1.6 copy.44
  227.5 0.0 all-to-all-done
  227.5 0.4 fusion.4
  227.9 0.7 copy.51
  228.6 4.1 %copy.54 = bf16[1,7168,256]{2,1,0:T(8,128)(2,1)} copy(bf16[1,7168,256]{2,1,0:T(8,128)(2,1)} %bitcast.29) | data formatting | bytes 7340032
  (11 shorter events, 0.0 us)
Async XLA Ops:
  0.6 226.9 %copy-start = (bf16[16,512,128]{2,1,0:T(8,128)(2,1)S(1)}, bf16[16,512,128]{2,1,0:T(8,128)(2,1)}, u32[]{:S(2)}) copy-start(bf16[16,512,128]{2,1,0:T(8,128)(2,1)} %param.16) | copy-start | bytes 6291460
  6.4 10.1 %copy-start.3 = (bf16[1792]{0:T(1024)(128)(2,1)S(1)}, bf16[1792]{0:T(1024)(128)(2,1)}, u32[]{:S(2)}) copy-start(bf16[1792]{0:T(1024)(128)(2,1)} %param.18) | copy-start | bytes 10756
  6.4 10.1 %copy-start.2 = (s32[32,8]{0,1:T(8,128)S(1)}, s32[32,8]{0,1:T(8,128)}, u32[]{:S(2)}) copy-start(s32[32,8]{0,1:T(8,128)} %param.20) | copy-start | bytes 3076
  6.4 10.2 %copy-start.1 = (bf16[32,1792]{1,0:T(8,128)(2,1)S(1)}, bf16[32,1792]{1,0:T(8,128)(2,1)}, u32[]{:S(2)}) copy-start(bf16[32,1792]{1,0:T(8,128)(2,1)} %param.17) | copy-start | bytes 344068
  6.4 10.3 %copy-start.5 = (s32[8]{0:T(128)S(1)}, s32[8]{0:T(128)}, u32[]{:S(2)}) copy-start(s32[8]{0:T(128)} %param.22) | copy-start | bytes 100
  6.5 10.3 %copy-start.6 = (s32[8]{0:T(128)S(1)}, s32[8]{0:T(128)}, u32[]{:S(2)}) copy-start(s32[8]{0:T(128)} %param.21) | copy-start | bytes 100
  12.4 215.1 %all-to-all-start = ((bf16[8,64,512]{2,0,1:T(8,128)(2,1)}), bf16[8,64,512]{2,0,1:T(8,128)(2,1)S(1)}, u32[]{:S(2)}, u32[]{:S(2)}) async-start(bf16[8,64,512]{2,0,1:T(8,128)(2,1)} %copy.36), calls=%async_computation | async-start | bytes 1048576 | tf_op jit(solution)/shard_map/all_to_all | solution.py:395
  18.1 7.2 %copy-start.4 = (s32[32,8]{0,1:T(8,128)S(1)}, s32[32,8]{0,1:T(8,128)}, u32[]{:S(2)}) copy-start(s32[32,8]{0,1:T(8,128)} %param.19) | copy-start | bytes 3076

commit v3 on v2

--- a/solution.py
+++ b/solution.py
@@ -72,6 +72,7 @@
     up_w,
     down_w,
     parts,
+    mid,
     came,
     acts,
     total,
@@ -157,7 +158,6 @@
             chosen_ref.at[to], held_ref.at[i], held_send.at[k], held_recv.at[i], to, t
         )
 
-    each(1, devices, lambda k: held_copy(k).start())
 
     home = i // per
 
@@ -186,12 +186,55 @@
 
     each(0, entries, project)
 
+    half = devices // 2
+    group, side = i // 2, lax.rem(i, 2)
+    pair = group * 2 + 1 - side
+
     def part_copy(k):
-        to = lax.rem(i + k, devices)
-        return remote(parts.at[to], came.at[i], part_send.at[k], part_recv.at[i], to, t)
-
-    each(1, devices, lambda k: part_copy(k).start())
-    came[i] = parts[i]
+        line = lax.rem(group + k, half)
+        return remote(
+            parts.at[line * 2 + 1 - side],
+            mid.at[line],
+            part_send.at[k],
+            part_recv.at[line],
+            pair,
+            t,
+        )
+
+    each(1, half, lambda k: part_copy(k).start())
+    part_copy(0).start()
+
+    def sum_copy(k):
+        mine = lax.rem(group + k, half) * 2 + side
+        return remote(
+            parts.at[mine],
+            came.at[group],
+            part_send.at[half + k],
+            part_recv.at[half + group],
+            mine,
+            t,
+        )
+
+    def part_sum(k):
+        line = lax.rem(group + k, half)
+        mine = line * 2 + side
+        remote(
+            parts.at[0], mid.at[line], part_send.at[0], part_recv.at[line], pair, t
+        ).wait_recv()
+
+        def add(e):
+            both = parts[mine, :, e].astype(jnp.float32) + mid[line, :, e].astype(jnp.float32)
+            parts[mine, :, e] = both.astype(jnp.bfloat16)
+
+        each(0, entries, add)
+
+    def part_pass(k):
+        part_sum(k)
+        sum_copy(k).start()
+
+    each(1, half, part_pass)
+    part_sum(0)
+    came[group] = parts[i]
 
     def square_arrival(k):
         origin = lax.rem(t + k, lanes)
@@ -204,12 +247,17 @@
     row_scale = lax.rsqrt(jnp.sum(squares[...], axis=0) / features + NORM_EPSILON)[:, :1]
 
     def part_arrival(k):
-        origin = lax.rem(i + k, devices)
-        remote(
-            parts.at[0], came.at[origin], part_send.at[0], part_recv.at[origin], origin, t
-        ).wait_recv()
-
-    each(1, devices, part_arrival)
+        line = lax.rem(group + k, half)
+        remote(
+            parts.at[0],
+            came.at[line],
+            part_send.at[0],
+            part_recv.at[half + line],
+            line * 2 + side,
+            t,
+        ).wait_recv()
+
+    each(1, half, part_arrival)
 
     def activate(e):
         gate = jnp.sum(came[:, 0, e].astype(jnp.float32), axis=0) * row_scale
@@ -220,19 +268,31 @@
     each(0, entries, activate)
 
     def act_copy(k):
-        to = lax.rem(i + k, devices)
+        to = lax.rem(group + k, half) * 2 + side
         return remote(acts.at[i], acts.at[i], act_send.at[k], act_recv.at[i], to, t)
 
-    each(1, devices, lambda k: act_copy(k).start())
+    def pair_copy(k):
+        origin = lax.rem(group + k, half) * 2 + side
+        return remote(
+            acts.at[origin], acts.at[origin], act_send.at[half + k], act_recv.at[origin], pair, t
+        )
+
+    each(1, half, lambda k: act_copy(k).start())
+    pair_copy(0).start()
+    each(1, devices, lambda k: held_copy(k).start())
+
+    def act_arrival(origin):
+        remote(
+            acts.at[i], acts.at[origin], act_send.at[0], act_recv.at[origin], pair, t
+        ).wait_recv()
+
+    def act_pass(k):
+        act_arrival(lax.rem(group + k, half) * 2 + side)
+        pair_copy(k).start()
+
+    each(1, half, act_pass)
     loads[2].wait()
-
-    def act_arrival(k):
-        origin = lax.rem(i + k, devices)
-        remote(
-            acts.at[i], acts.at[origin], act_send.at[0], act_recv.at[origin], origin, t
-        ).wait_recv()
-
-    each(1, devices, act_arrival)
+    each(0, half, lambda k: act_arrival(lax.rem(group + k, half) * 2 + 1 - side))
     total[...] = jnp.zeros_like(total)
 
     def lower(e):
@@ -279,8 +339,10 @@
         each(1, lanes, lambda k, p=p: row_copy(p, k).wait_send())
         pl.when(t * per + p != i)(lambda p=p: row_copy(p, 0).wait_send())
     each(1, lanes, lambda k: square_copy(k).wait_send())
-    each(1, devices, lambda k: part_copy(k).wait_send())
-    each(1, devices, lambda k: act_copy(k).wait_send())
+    each(0, half, lambda k: part_copy(k).wait_send())
+    each(1, half, lambda k: sum_copy(k).wait_send())
+    each(1, half, lambda k: act_copy(k).wait_send())
+    each(0, half, lambda k: pair_copy(k).wait_send())
     each(1, devices, lambda k: back_copy(k).wait_send())
     pl.when(home != t)(lambda: back_copy(0).wait_send())
 
@@ -318,7 +380,8 @@
             pltpu.VMEM(up.shape, bf16),
             pltpu.VMEM(down.shape, bf16),
             pltpu.VMEM((devices, 2, entries, row_count, width), bf16),
-            pltpu.VMEM((devices, 2, entries, row_count, width), bf16),
+            pltpu.VMEM((devices // 2, 2, entries, row_count, width), bf16),
+            pltpu.VMEM((devices // 2, 2, entries, row_count, width), bf16),
             pltpu.VMEM((devices, entries, row_count, width), bf16),
             pltpu.VMEM((devices * row_count, depth), jnp.float32),
             pltpu.VMEM((devices, row_count, depth), bf16),

time: 236 us -> 199 us (0.84); the launches traced: 233 us -> 198 us
  Pallas kernels: 206 us -> 172 us
    pallas_call x1, Pallas kernels: 199 us -> 165 us  [moe(): pl.pallas_call(functools.partial(moe_kernel, devices, lanes), out_shape=(...]
  transfers between devices with their start and end apart: 1 -> 1, of which waited for: 0 -> 0; matrix products, arithmetic and copies ran while one was open for 2% -> 2% of each run, Pallas kernels for 89% -> 87%
where the time goes in v3:
time: 199 us; the launch traced here: 198 us
  Pallas kernels  172 us (86%)
  matrix products  10.2 us (5%)
  local copies, waits for them, and re-layouts  9.61 us (5%)
  starting transfers between devices  4.11 us (2%)
    pallas_call x1, Pallas kernels, moe(): pl.pallas_call(functools.partial(moe_kernel, devices, lanes), out_shape=(...  165 us
    pallas_call x1, Pallas kernels, pick_entries(): pl.pallas_call(copy, grid_spec=pltpu.PrefetchScalarGridSpec(num_scalar_pr...  7.16 us
    sub x1, matrix products, attend(): lifted = jnp.where(allowed, jnp.exp(scores - highest), 0.0)  4.89 us
    dot_general x1, matrix products, attend(): jnp.einsum('rhp,rpc->rhc', lifted.astype(jnp.bfloat16), kv_cache[:, :, :K...  4.85 us
    unnamed x15, local copies, waits for them, and re-layouts  4.15 us
    all_to_all x1, starting transfers between devices, per_device(): lax.all_to_all(latent, 'tensor', split_axis=1, concat_axis=0, tiled=True)  4.11 us
  transfers between devices with their start and end apart: 1, of which 0 were waited for; matrix products, arithmetic and copies ran while one was open for 2% of the time, Pallas kernels for 87%

profile of v3, /device:TPU:27, one launch (start us, length us, event | category | flops | bytes accessed | tf_op | source)
XLA Modules:
  0.0 198.5 jit_solution(6392681927159884085)
XLA Ops:
  0.6 0.0 copy-start
  0.6 0.9 iota_compare_fusion
  1.5 4.9 %fusion.12 = (f32[8,64]{1,0:T(8,128)S(1)}, bf16[8,64,768]{2,1,0:T(8,128)(2,1)S(1)}) fusion(pred[8,768]{1,0:T(8,128)(4,1)S(1)} %iota_compare_fusion, bf16[8,64,576]{2,1,0:T(8,128)(2,1)} %param.13, bf16[8,768,576]{1,2,0:T(8,128)(2,1)} %param.14), kind=kOutput, calls=%fused_computation.23 | convolution fusion | flops 455344896 | bytes 8462336 | tf_op jit(solution)/shard_map/sub | solution.py:28
  6.4 0.0 copy-start.3
  6.4 0.0 copy-start.2
  6.4 0.0 copy-start.1
  6.4 0.0 copy-start.5
  6.5 0.0 copy-start.6
  6.5 4.9 %divide_convert_fusion = bf16[8,64,512]{2,1,0:T(8,128)(2,1)S(1)} fusion(bf16[8,768,576]{1,2,0:T(8,128)(2,1)} %param.14, bf16[8,64,768]{2,1,0:T(8,128)(2,1)S(1)} %get-tuple-element.10, f32[8,64]{1,0:T(8,128)S(1)} %get-tuple-element.9), kind=kOutput, calls=%fused_computation.8 | convolution fusion | flops 403177472 | bytes 7604224 | tf_op jit(solution)/shard_map/rhp,rpc->rhc/dot_general | solution.py:30
  11.3 1.1 copy.36
  12.4 4.1 %all-to-all-start = ((bf16[8,64,512]{2,0,1:T(8,128)(2,1)}), bf16[8,64,512]{2,0,1:T(8,128)(2,1)S(1)}, u32[]{:S(2)}, u32[]{:S(2)}) async-start(bf16[8,64,512]{2,0,1:T(8,128)(2,1)} %copy.36), calls=%async_computation | async-start | bytes 1048576 | tf_op jit(solution)/shard_map/all_to_all | solution.py:458
  16.6 0.1 fusion.11
  16.8 0.7 select_reduce_fusion.1.entries_ref
  17.5 0.7 copy.52
  18.1 7.2 %shard_map.148 = bf16[8,896,256]{2,1,0:T(8,128)(2,1)} custom-call(s32[8]{0:T(128)} %select_reduce_fusion.1.entries_ref, bf16[8,896,256]{2,1,0:T(8,128)(2,1)} %gate_hbm.1), custom_call_target="tpu_custom_call" | custom-call | tf_op jit(solution)/shard_map/pallas_call | solution.py:45
  25.3 0.1 select_reduce_fusion
  25.4 0.7 broadcast_in_dim.21.square_ref
  26.0 0.8 broadcast_in_dim.22.share_ref
  26.8 164.9 %shard_map.149 = (bf16[2,32,896]{2,1,0:T(8,128)(2,1)}, bf16[8,1,896,256]{3,2,1,0:T(8,128)(2,1)}) custom-call(bf16[2,32,896]{2,1,0:T(8,128)(2,1)} %bitcast.31, f32[32,128]{1,0:T(8,128)} %broadcast_in_dim.21.square_ref, f32[8,32,256]{2,1,0:T(8,128)} %broadcast_in_dim.22.share_ref, bf16[8,1,896,256]{3,2,1,0:T(8,128)(2,1)} %bitcast.28, ...), custom_call_target="tpu_custom_call" | custom-call | flops 2818572288 | bytes 18350080 | tf_op jit(solution)/shard_map/pallas_call | solution.py:368
  191.7 1.6 copy.44
  193.3 0.0 all-to-all-done
  193.3 0.4 fusion.4
  193.7 0.7 copy.51
  194.4 4.1 %copy.54 = bf16[1,7168,256]{2,1,0:T(8,128)(2,1)} copy(bf16[1,7168,256]{2,1,0:T(8,128)(2,1)} %bitcast.29) | data formatting | bytes 7340032
  (11 shorter events, 0.0 us)
Async XLA Ops:
  0.6 192.6 %copy-start = (bf16[16,512,128]{2,1,0:T(8,128)(2,1)S(1)}, bf16[16,512,128]{2,1,0:T(8,128)(2,1)}, u32[]{:S(2)}) copy-start(bf16[16,512,128]{2,1,0:T(8,128)(2,1)} %param.16) | copy-start | bytes 6291460
  6.4 10.1 %copy-start.3 = (bf16[1792]{0:T(1024)(128)(2,1)S(1)}, bf16[1792]{0:T(1024)(128)(2,1)}, u32[]{:S(2)}) copy-start(bf16[1792]{0:T(1024)(128)(2,1)} %param.18) | copy-start | bytes 10756
  6.4 10.1 %copy-start.2 = (s32[32,8]{0,1:T(8,128)S(1)}, s32[32,8]{0,1:T(8,128)}, u32[]{:S(2)}) copy-start(s32[32,8]{0,1:T(8,128)} %param.20) | copy-start | bytes 3076
  6.4 10.2 %copy-start.1 = (bf16[32,1792]{1,0:T(8,128)(2,1)S(1)}, bf16[32,1792]{1,0:T(8,128)(2,1)}, u32[]{:S(2)}) copy-start(bf16[32,1792]{1,0:T(8,128)(2,1)} %param.17) | copy-start | bytes 344068
  6.4 10.3 %copy-start.5 = (s32[8]{0:T(128)S(1)}, s32[8]{0:T(128)}, u32[]{:S(2)}) copy-start(s32[8]{0:T(128)} %param.22) | copy-start | bytes 100
  6.5 10.3 %copy-start.6 = (s32[8]{0:T(128)S(1)}, s32[8]{0:T(128)}, u32[]{:S(2)}) copy-start(s32[8]{0:T(128)} %param.21) | copy-start | bytes 100
  12.4 180.8 %all-to-all-start = ((bf16[8,64,512]{2,0,1:T(8,128)(2,1)}), bf16[8,64,512]{2,0,1:T(8,128)(2,1)S(1)}, u32[]{:S(2)}, u32[]{:S(2)}) async-start(bf16[8,64,512]{2,0,1:T(8,128)(2,1)} %copy.36), calls=%async_computation | async-start | bytes 1048576 | tf_op jit(solution)/shard_map/all_to_all | solution.py:458
  18.1 7.2 %copy-start.4 = (s32[32,8]{0,1:T(8,128)S(1)}, s32[32,8]{0,1:T(8,128)}, u32[]{:S(2)}) copy-start(s32[32,8]{0,1:T(8,128)} %param.19) | copy-start | bytes 3076
